TPU v7x, 256 devices: a whole 4x4x8 slice. The times are simulated.
256 devices in a mesh: tm: 8 (over z_lo, core), sub: 32 (over z_hi, y, x).
Axes of the slice: x: 4, y: 4, z: 8 (z_hi: 2, z_lo: 4; z = z_hi * 4 + z_lo), core: 2. Of those that a mesh axis runs over, the one named last changes fastest.
Arguments:
- field_grads: bfloat16 [8, 3, 1024, 128, 128], P('tm', None, None, 'sub'), may hold values from -6 to 6
- model: float32 [8, 128, 128], P('tm', 'sub'), may hold values from -6 to 6
- observed: float32 [8, 1024, 1024], P('tm', 'sub'), may hold values from -6 to 6
- data_weight: float32 [8, 1024, 1024], P('tm', 'sub'), may hold values from 0.3 to 3
Outputs:
- misfit: float32 [8, 1024, 1024], P('tm', 'sub')
- gradient: float32 [8, 128, 128], P('tm', 'sub')
All inputs are finite; a program needn't handle non-finite values.
Results may differ from a plain program's by a relative error of at most 0.0021.
Values may be sent and summed in bfloat16 or wider, within the bound.
A program may use at most 64 MiB of HBM per device.

v0:
```python
import jax
import jax.numpy as jnp
from jax import lax
from jax.sharding import PartitionSpec as P


def padded_2(array, sides, width):
    for axis, dim in sides:
        devices, length = (lax.axis_size(axis), array.shape[dim])
        up = [(i, (i + 1) % devices) for i in range(devices - 1)]
        down = [(j, i) for i, j in up]
        last = lax.slice_in_dim(array, length - width, length, axis=dim)
        first = lax.slice_in_dim(array, 0, width, axis=dim)
        before = lax.ppermute(last, axis, up)
        after = lax.ppermute(first, axis, down)
        array = jnp.concatenate([before, array, after], axis=dim)
    return array


def body(field_grads, model, observed, data_weight):
    electrodes = field_grads.shape[2]
    columns = field_grads.shape[3]
    width = field_grads.shape[4]
    local_cells = columns * width
    parts = lax.axis_size("sub")
    own_rows = electrodes // parts
    scale = 1.0 / jnp.sqrt(jnp.float32(3 * local_cells * parts))
    grads_flat = field_grads.reshape(3, electrodes, local_cells)
    cells = model.reshape(local_cells)
    weighted = (grads_flat.astype(jnp.float32) * cells).astype(jnp.bfloat16)
    total = jnp.zeros((electrodes, electrodes), jnp.float32)
    for k in range(3):
        rows_k = weighted[k]
        total = total + lax.dot_general(
            rows_k, grads_flat[k], (((1,), (1,)), ((), ())), preferred_element_type=jnp.float32
        )
    whole = lax.psum(total, "sub")
    mine = lax.dynamic_slice_in_dim(whole, lax.axis_index("sub") * own_rows, own_rows, 0)
    predicted = mine * scale
    misfit = data_weight[0] * (predicted - observed[0])
    back = (data_weight[0] * misfit).astype(jnp.bfloat16)
    carry = jnp.zeros((local_cells,), jnp.float32)
    piece = lax.all_gather(back, "sub", axis=0, tiled=True)
    for k in range(3):
        product = jnp.dot(piece, grads_flat[k], preferred_element_type=jnp.float32)
        rows_k = grads_flat[k]
        carry = carry + jnp.sum(rows_k.astype(jnp.float32) * product, axis=0)
    padded = padded_2(model, (("tm", 0), ("sub", 1)), 1)
    centre = padded[1:2, 1:-1, :]
    beside = padded[2:3, 1:-1, :] + padded[0:1, 1:-1, :]
    beside = beside + padded[1:2, 2:, :] + padded[1:2, :-2, :]
    side_pad = jnp.pad(centre, ((0, 0), (0, 0), (1, 1)))
    beside = beside + side_pad[:, :, 2:] + side_pad[:, :, :-2]
    gradient = (carry * scale).reshape(1, columns, width) + 6.0 * centre - beside
    return (misfit.reshape(1, own_rows, electrodes), gradient)


def solution(mesh):
    return jax.shard_map(
        body,
        mesh=mesh,
        in_specs=(
            P("tm", None, None, "sub", None),
            P("tm", "sub", None),
            P("tm", "sub", None),
            P("tm", "sub", None),
        ),
        out_specs=(P("tm", "sub", None), P("tm", "sub", None)),
        check_vma=False,
    )
```

profile of v0, /device:TPU:2, one launch (start us, length us, event | category | flops | bytes accessed | tf_op | source)
XLA Modules:
  0.0 585.8 jit_solution(4255853890342397425)
XLA Ops:
  7.2 0.0 all-reduce.3.cloned.1.call-start
  7.2 4.5 fusion.22
  11.7 3.8 reshape.53
  15.5 3.8 multiply_convert_fusion
  19.3 1.3 fusion.3
  20.6 1.3 fusion.6
  21.9 3.4 add_add_fusion
  25.2 0.0 all-reduce.3.cloned.1.call-update
  25.3 0.0 all-gather.2.cloned.1.call-start
  25.3 452.9 %all-reduce.3.cloned.1.call-done = f32[1024,1024]{1,0:T(8,128)} async-done(((f32[1024,1024]{1,0:T(8,128)}), f32[1024,1024]{1,0:T(8,128)}) %all-reduce.3.cloned.1.call-update) | async-done | bytes 4194320 | tf_op jit(solution)/shard_map/psum | solution.py:37
  478.2 1.6 fusion.15
  479.8 0.0 all-gather.2.cloned.1.call-update
  479.8 1.3 collective-permute-start.1
  481.1 1.3 collective-permute-start
  482.4 2.6 collective-permute-done
  485.1 2.5 collective-permute-start.2
  487.6 3.4 collective-permute-start.3
  490.9 81.8 %all-gather.2.cloned.1.call-done = bf16[1024,1024]{1,0:T(8,128)(2,1)} async-done(((bf16[32,1024]{1,0:T(8,128)(2,1)}), bf16[1024,1024]{1,0:T(8,128)(2,1)}) %all-gather.2.cloned.1.call-update) | async-done | bytes 2097168 | tf_op jit(solution)/shard_map/all_gather | solution.py:43
  572.7 3.0 multiply_reduce_fusion.1
  575.7 1.3 multiply_reduce_fusion.2
  577.0 1.3 multiply_reduce_fusion
  578.3 0.0 collective-permute-done.2
  578.3 0.0 collective-permute-done.3
  578.3 0.7 fusion.19
  (21 shorter events, 0.1 us)
Async XLA Ops:
  7.2 4.5 copy-start
  7.2 471.0 %all-reduce.3.cloned.1.call-start = ((), (), s32[]{:S(2)}) async-start(), calls=%async_computation | async-start | bytes 8388608 | tf_op jit(solution)/shard_map/psum | solution.py:37
  11.7 3.8 copy-start.6
  15.5 3.8 copy-start.3
  19.2 1.3 copy-start.2
  20.6 1.3 copy-start.1
  25.2 452.9 %copy-start.4 = (f32[1,32,1024]{2,1,0:T(8,128)S(1)}, f32[1,32,1024]{2,1,0:T(8,128)}, u32[]{:S(2)}) copy-start(f32[1,32,1024]{2,1,0:T(8,128)} %param.7) | copy-start | bytes 393220
  25.2 452.9 %copy-start.5 = (f32[1,32,1024]{2,1,0:T(8,128)S(1)}, f32[1,32,1024]{2,1,0:T(8,128)}, u32[]{:S(2)}) copy-start(f32[1,32,1024]{2,1,0:T(8,128)} %param.6) | copy-start | bytes 393220
  25.3 547.5 %all-gather.2.cloned.1.call-start = ((), (), s32[]{:S(2)}) async-start(), calls=%async_computation.1 | async-start | bytes 2162688 | tf_op jit(solution)/shard_map/all_gather | solution.py:43
  479.8 2.6 collective-permute-start.1
  481.1 4.0 collective-permute-start
  485.1 93.2 %collective-permute-start.2 = (f32[3,1,128]{2,1,0:T(1,128)S(1)}, f32[3,1,128]{2,1,0:T(1,128)S(1)}, u32[]{:S(2)}, u32[]{:S(2)}) collective-permute-start(f32[3,1,128]{2,1,0:T(1,128)S(1)} %get-tuple-element.7), channel_id=1, source_target_pairs={{1,0},{2,1},{3,2},{4,3},{5,4},{6,5},{7,6},{8,7},{9,8},{10,9},{11,1... | collective-permute-start | bytes 4616 | tf_op jit(solution)/shard_map/ppermute | solution.py:15
  487.6 90.7 %collective-permute-start.3 = (f32[3,1,128]{2,1,0:T(1,128)S(1)}, f32[3,1,128]{2,1,0:T(1,128)S(1)}, u32[]{:S(2)}, u32[]{:S(2)}) collective-permute-start(f32[3,1,128]{2,1,0:T(1,128)S(1)} %get-tuple-element.8), channel_id=1, source_target_pairs={{0,1},{1,2},{2,3},{3,4},{4,5},{5,6},{6,7},{7,8},{8,9},{9,10},{10,1... | collective-permute-start | bytes 4616 | tf_op jit(solution)/shard_map/ppermute | solution.py:14
  572.7 3.0 copy-start.7
Sparse Core Ops, SparseCore 0:
  25.4 452.7 all-reduce.2
  481.7 90.9 all-gather.1
where the time goes:
time: 586 us
  waiting for transfers between devices  537 us (92%)
  between operations  14.2 us (2%)
  matrix products  11.5 us (2%)
  starting transfers between devices  8.49 us (1%)
  local copies, waits for them, and re-layouts  8.3 us (1%)
  other arithmetic  6 us (1%)
    psum x1, waiting for transfers between devices, body(): whole = lax.psum(total, 'sub')  453 us
    all_gather x1, waiting for transfers between devices, body(): piece = lax.all_gather(back, 'sub', axis=0, tiled=True)  81.8 us
  transfers between devices with their start and end apart: 6, of which 3 were waited for; matrix products, arithmetic and copies ran while one was open for 1% of the time, Pallas kernels for 0%

commit v1 on v0

v1 whole, which is shorter than its diff:
```python
import jax
import jax.numpy as jnp
from jax import lax
from jax.experimental import pallas as pl
from jax.experimental.pallas import tpu as pltpu
from jax.sharding import PartitionSpec as P

MESH = pl.DeviceIdType.MESH
F32 = jnp.float32
BF16 = jnp.bfloat16
NX = 4
NY = 4
NZ = 2


def remote(src, dst, send, recv, peer):
    return pltpu.make_async_remote_copy(
        src_ref=src,
        dst_ref=dst,
        send_sem=send,
        recv_sem=recv,
        device_id=peer,
        device_id_type=MESH,
    )


def kernel(
    grads,
    weighted,
    model,
    observed,
    weight,
    misfit_out,
    gradient_out,
    send1,
    recv1,
    acc1,
    recv2,
    acc2,
    recv3,
    gather_a,
    gather_b,
    total,
    faces,
    s1,
    r1,
    s2,
    r2,
    s3,
    r3,
    sf,
    rf,
):
    electrodes, terms = grads.shape
    half = electrodes // 2
    own = misfit_out.shape[1]
    group = NZ * own
    chunk = 4 * group
    cells = terms // 3
    parts = NX * NY * NZ
    tm = lax.axis_index("tm")
    sub = lax.axis_index("sub")
    times = lax.axis_size("tm")
    x = lax.rem(sub, NX)
    y = lax.rem(sub // NX, NY)
    z = sub // (NX * NY)

    def at(zz, yy, xx):
        return {"sub": (zz * NY + yy) * NX + xx}

    def x_peer(d):
        return at(z, y, lax.rem(x + d, NX))

    def y_peer(d):
        return at(z, lax.rem(y + d, NY), x)

    z_peer = at(1 - z, y, x)
    beside = (
        {"tm": lax.rem(tm + 1, times)},
        {"tm": lax.rem(tm + times - 1, times)},
        {"sub": lax.rem(sub + 1, parts)},
        {"sub": lax.rem(sub + parts - 1, parts)},
    )

    barrier = pltpu.get_barrier_semaphore()
    peers = [x_peer(d) for d in (1, 2, 3)] + [y_peer(d) for d in (1, 2, 3)]
    peers += [z_peer] + list(beside)
    for peer in peers:
        pl.semaphore_signal(barrier, inc=1, device_id=peer, device_id_type=MESH)
    pl.semaphore_wait(barrier, len(peers))

    face_copies = [
        remote(model.at[0], faces.at[n], sf.at[n], rf.at[n], peer)
        for n, peer in enumerate(beside)
    ]
    for copy in face_copies:
        copy.start()

    def rows_of(yy, xx, zz):
        return pl.ds(pl.multiple_of(((zz * NY + yy) * NX + xx) * own, own), own)

    def part(pieces, columns):
        rows = jnp.concatenate([weighted[p, :] for p in pieces], axis=0)
        return lax.dot_general(
            rows, grads[columns, :], (((1,), (1,)), ((), ())), preferred_element_type=F32
        )

    def part_a(xx):
        pieces = [rows_of(yy, xx, zz) for yy in range(NY) for zz in range(NZ)]
        return part(pieces, slice(0, half))

    def part_b(yy):
        pieces = [rows_of(yy, xx, zz) for xx in range(NX) for zz in range(NZ)]
        return part(pieces, slice(half, electrodes))

    first = {}
    for d in (2, 1, 3):
        send1[0, d - 1] = part_a(lax.rem(x + d, NX)).astype(BF16)
        first[0, d] = remote(send1.at[0, d - 1], recv1.at[0, d - 1], s1.at[0, d - 1], r1.at[0, d - 1], x_peer(d))
        first[0, d].start()
        send1[1, d - 1] = part_b(lax.rem(y + d, NY)).astype(BF16)
        first[1, d] = remote(send1.at[1, d - 1], recv1.at[1, d - 1], s1.at[1, d - 1], r1.at[1, d - 1], y_peer(d))
        first[1, d].start()
    acc1[0] = part_a(x)
    acc1[1] = part_b(y)

    second = {}
    for h, mine, peer_of in ((0, y, y_peer), (1, x, x_peer)):
        for d in (1, 3, 2):
            first[h, d].wait_recv()
        acc1[h] += recv1[h, 0].astype(F32) + recv1[h, 1].astype(F32) + recv1[h, 2].astype(F32)
        for d in (2, 1, 3):
            other = lax.rem(mine + d, 4)
            src = acc1.at[h, pl.ds(pl.multiple_of(other * group, group), group), :]
            second[h, d] = remote(src, recv2.at[h, d - 1], s2.at[h, d - 1], r2.at[h, d - 1], peer_of(d))
            second[h, d].start()
    third = {}
    for h, mine in ((0, y), (1, x)):
        for d in (1, 3, 2):
            second[h, d].wait_recv()
        kept = acc1[h, pl.ds(pl.multiple_of(mine * group, group), group), :]
        acc2[h] = kept + recv2[h, 0] + recv2[h, 1] + recv2[h, 2]
        src = acc2.at[h, pl.ds(pl.multiple_of((1 - z) * own, own), own), :]
        third[h] = remote(src, recv3.at[h], s3.at[h], r3.at[h], z_peer)
        third[h].start()

    scale = 1.0 / jnp.sqrt(F32(cells * 3 * parts))
    gather = (gather_a, gather_b)
    slots = ((y, x), (x, y))
    copies = []
    level0 = {}
    for h in range(2):
        third[h].wait_recv()
        columns = slice(h * half, (h + 1) * half)
        summed = acc2[h, pl.ds(pl.multiple_of(z * own, own), own), :] + recv3[h]
        w = weight[0, :, columns]
        misfit = w * (summed * scale - observed[0, :, columns])
        misfit_out[0, :, columns] = misfit
        block = gather[h].at[slots[h][0], slots[h][1], z]
        block[...] = (w * misfit).astype(BF16)
        level0[h] = remote(block, block, s3.at[2 + h], r3.at[2 + h], z_peer)
        level0[h].start()

    level1 = {}
    for h, peer_of in ((0, x_peer), (1, y_peer)):
        level0[h].wait_recv()
        for d in (2, 1, 3):
            block = gather[h].at[slots[h][0], slots[h][1]]
            level1[h, d] = remote(block, block, s2.at[2 + h, d - 1], r2.at[2 + h, d - 1], peer_of(d))
            level1[h, d].start()
    level2 = {}
    for h, peer_of in ((0, y_peer), (1, x_peer)):
        for d in (1, 3, 2):
            level1[h, d].wait_recv()
        for d in (2, 1, 3):
            block = gather[h].at[slots[h][0]]
            level2[h, d] = remote(block, block, s1.at[2 + h, d - 1], r1.at[2 + h, d - 1], peer_of(d))
            level2[h, d].start()

    total[...] = jnp.zeros_like(total)

    def add(h, slot):
        back = gather[h][slot].reshape(chunk, half)
        product = jnp.dot(back, grads[h * half : (h + 1) * half, :], preferred_element_type=F32)
        outer = range(4)
        if h == 0:
            pieces = [rows_of(slot, xx, zz) for xx in outer for zz in range(NZ)]
        else:
            pieces = [rows_of(yy, slot, zz) for yy in outer for zz in range(NZ)]
        rows = jnp.concatenate([grads[p, :] for p in pieces], axis=0)
        terms_of = product * rows.astype(F32)
        total[...] += jnp.sum(terms_of.reshape(chunk // 8, 8, terms), axis=0)

    add(0, y)
    add(1, x)
    for d in (1, 3, 2):
        for h, mine in ((0, y), (1, x)):
            level2[h, d].wait_recv()
            add(h, lax.rem(mine + 4 - d, 4))

    for copy in face_copies:
        copy.wait_recv()
    centre = model[0]
    lane = lax.broadcasted_iota(jnp.int32, centre.shape, 1)
    width = centre.shape[1]
    row = lax.broadcasted_iota(jnp.int32, centre.shape, 0)
    height = centre.shape[0]
    nil = jnp.zeros_like(centre)
    before_t = jnp.where(tm > 0, faces[0], nil)
    after_t = jnp.where(tm < times - 1, faces[1], nil)
    before_s = jnp.where(sub > 0, faces[2], nil)
    after_s = jnp.where(sub < parts - 1, faces[3], nil)
    near = after_t + before_t
    near = near + jnp.concatenate([centre[1:], after_s[:1]], axis=0)
    near = near + jnp.concatenate([before_s[height - 1 :], centre[: height - 1]], axis=0)
    near = near + jnp.where(lane == width - 1, 0.0, pltpu.roll(centre, width - 1, 1))
    near = near + jnp.where(lane == 0, 0.0, pltpu.roll(centre, 1, 1))
    smooth = 6.0 * centre - near
    flat = jnp.sum(total[...], axis=0, keepdims=True)
    flat = (flat[:, :cells] + flat[:, cells : 2 * cells] + flat[:, 2 * cells :]) * scale
    for j in range(height):
        gradient_out[0, j : j + 1, :] = flat[:, j * width : (j + 1) * width] + smooth[j : j + 1]

    for copy in face_copies:
        copy.wait_send()
    for sent in (first, second, third, level0, level1, level2):
        for copy in sent.values():
            copy.wait_send()


def body(field_grads, model, observed, data_weight):
    electrodes = field_grads.shape[2]
    columns = field_grads.shape[3]
    width = field_grads.shape[4]
    cells = columns * width
    own = observed.shape[1]
    half = electrodes // 2
    group = NZ * own
    chunk = 4 * group
    grads = jnp.transpose(field_grads[0], (1, 0, 2, 3)).reshape(electrodes, 3 * cells)
    m = jnp.tile(model.reshape(1, cells), (1, 3))
    weighted = (grads.astype(F32) * m).astype(BF16)
    dma = pltpu.SemaphoreType.DMA
    vmem = pl.BlockSpec(memory_space=pltpu.VMEM)
    return pl.pallas_call(
        kernel,
        out_shape=(
            jax.ShapeDtypeStruct(observed.shape, F32),
            jax.ShapeDtypeStruct(model.shape, F32),
        ),
        in_specs=[vmem] * 5,
        out_specs=(vmem, vmem),
        scratch_shapes=[
            pltpu.VMEM((2, 3, chunk, half), BF16),
            pltpu.VMEM((2, 3, chunk, half), BF16),
            pltpu.VMEM((2, chunk, half), F32),
            pltpu.VMEM((2, 3, group, half), F32),
            pltpu.VMEM((2, group, half), F32),
            pltpu.VMEM((2, own, half), F32),
            pltpu.VMEM((4, 4, NZ, own, half), BF16),
            pltpu.VMEM((4, 4, NZ, own, half), BF16),
            pltpu.VMEM((8, 3 * cells), F32),
            pltpu.VMEM((4, columns, width), F32),
            dma((4, 3)),
            dma((4, 3)),
            dma((4, 3)),
            dma((4, 3)),
            dma((4,)),
            dma((4,)),
            dma((4,)),
            dma((4,)),
        ],
        compiler_params=pltpu.CompilerParams(
            collective_id=0, has_side_effects=True, vmem_limit_bytes=48 * 1024 * 1024
        ),
    )(grads, weighted, model, observed, data_weight)


def solution(mesh):
    return jax.shard_map(
        body,
        mesh=mesh,
        in_specs=(
            P("tm", None, None, "sub", None),
            P("tm", "sub", None),
            P("tm", "sub", None),
            P("tm", "sub", None),
        ),
        out_specs=(P("tm", "sub", None), P("tm", "sub", None)),
        check_vma=False,
    )
```

time: 586 us -> 83.1 us (0.14)
  the two profiles are of different devices: /device:TPU:2 before, /device:TPU:34 now
where the time goes in v1:
time: 83.1 us; the launch traced here: 82.8 us
  Pallas kernels  68.6 us (83%)
  local copies, waits for them, and re-layouts  11.3 us (14%)
  other arithmetic  2.27 us (3%)
    pallas_call x1, Pallas kernels, body(): pl.pallas_call(kernel, out_shape=(jax.ShapeDtypeStruct(observed.shape, F3...  68.6 us
    reshape x1, local copies, waits for them, and re-layouts, body(): jnp.transpose(field_grads[0], (1, 0, 2, 3)).reshape(electrodes, 3 * cells)  4.73 us
    transpose x1, local copies, waits for them, and re-layouts, body(): jnp.transpose(field_grads[0], (1, 0, 2, 3)).reshape(electrodes, 3 * cells)  4.61 us
    convert_element_type x1, other arithmetic, body(): weighted = (grads.astype(F32) * m).astype(BF16)  2.27 us

profile of v1, /device:TPU:34, one launch (start us, length us, event | category | flops | bytes accessed | tf_op | source)
XLA Modules:
  0.0 82.8 jit_solution(16139318805690294509)
XLA Ops:
  0.6 0.7 tile.11
  1.3 4.6 %copy.6 = bf16[1024,3,4,128]{3,2,1,0:T(4,128)(2,1)} copy(bf16[1024,3,4,128]{3,2,0,1:T(4,128)(2,1)} %bitcast.5) | data formatting | bytes 6291456 | tf_op jit(solution)/shard_map/transpose | solution.py:240
  5.9 4.7 %reshape.13.grads = bf16[1024,1536]{1,0:T(8,128)(2,1)S(1)} reshape(bf16[1024,3,4,128]{3,2,1,0:T(4,128)(2,1)} %copy.6) | data formatting | bytes 6291456 | tf_op jit(solution)/shard_map/reshape | solution.py:240
  10.7 0.0 copy-start
  10.7 0.0 copy-start.1
  10.7 0.0 copy-start.2
  10.7 2.3 %multiply_convert_fusion.weighted = bf16[1024,1536]{1,0:T(8,128)(2,1)} fusion(bf16[1024,1536]{1,0:T(8,128)(2,1)S(1)} %reshape.13.grads, f32[1536]{0:T(1024)S(1)} %tile.12), kind=kLoop, calls=%fused_computation | loop fusion | flops 4718592 | bytes 6297600 | tf_op jit(solution)/shard_map/convert_element_type | solution.py:242
  13.0 0.0 copy-done
  13.0 0.0 copy-done.1
  13.0 0.0 copy-done.2
  13.0 68.6 %shard_map.59 = (f32[1,32,1024]{2,1,0:T(8,128)S(1)}, f32[1,4,128]{2,1,0:T(4,128)S(1)}) custom-call(bf16[1024,1536]{1,0:T(8,128)(2,1)S(1)} %reshape.13.grads, bf16[1024,1536]{1,0:T(8,128)(2,1)} %multiply_convert_fusion.weighted, f32[1,4,128]{2,1,0:T(4,128)S(1)} %copy-done.2, f32[1,32,1024]{2,1,0:T(8,128)S(1)} %copy-done, f32[1,32,1024]{2,1,0:T(8,128)S(1)} %copy-done.1), custom_call_target="tpu_custom_call" | custom-call | tf_op jit(solution)/shard_map/pallas_call | solution.py:245
  81.6 0.7 copy.9
  82.3 0.6 copy.10
  (1 shorter events, 0.0 us)
Async XLA Ops:
  10.7 2.3 %copy-start = (f32[1,32,1024]{2,1,0:T(8,128)S(1)}, f32[1,32,1024]{2,1,0:T(8,128)}, u32[]{:S(2)}) copy-start(f32[1,32,1024]{2,1,0:T(8,128)} %observed.1) | copy-start | bytes 393220
  10.7 2.3 %copy-start.1 = (f32[1,32,1024]{2,1,0:T(8,128)S(1)}, f32[1,32,1024]{2,1,0:T(8,128)}, u32[]{:S(2)}) copy-start(f32[1,32,1024]{2,1,0:T(8,128)} %weight.1) | copy-start | bytes 393220
  10.7 2.3 %copy-start.2 = (f32[1,4,128]{2,1,0:T(4,128)S(1)}, f32[1,4,128]{2,1,0:T(4,128)}, u32[]{:S(2)}) copy-start(f32[1,4,128]{2,1,0:T(4,128)} %model.1) | copy-start | bytes 6148

commit v2 on v0

v2 whole, which is shorter than its diff:
```python
import jax
import jax.numpy as jnp
from jax import lax
from jax.experimental import pallas as pl
from jax.experimental.pallas import tpu as pltpu
from jax.sharding import PartitionSpec as P

MESH = pl.DeviceIdType.MESH
F32 = jnp.float32
BF16 = jnp.bfloat16
N = 4
NZ = 2
LANES = 128
FAR_FIRST = (2, 1, 3)
NEAR_FIRST = (1, 3, 2)


def kernel(
    fields,
    model,
    observed,
    weight,
    misfit_out,
    gradient_out,
    raw,
    grads,
    weighted,
    pairs_a,
    pairs_b,
    send_a,
    send_b,
    recv_a,
    recv_b,
    acc_a,
    acc_b,
    recv_a2,
    recv_b2,
    z_send,
    z_recv,
    gather_a,
    gather_b,
    data,
    data_y,
    data_t,
    data_x,
    data_u,
    data_z,
    post,
    post_y,
    post_t,
    post_x,
    potential,
    total,
    faces,
    load_sem,
    send_sem,
    recv_sem,
):
    electrodes, terms = grads.shape
    half = electrodes // 2
    own = misfit_out.shape[1]
    tile = N * own
    cells = terms // 3
    parts = N * N * NZ
    tm = lax.axis_index("tm")
    sub = lax.axis_index("sub")
    times = lax.axis_size("tm")
    x = lax.rem(sub, N)
    y = lax.rem(sub // N, N)
    z = sub // (N * N)

    def at(zz, yy, xx):
        return {"sub": (zz * N + yy) * N + xx}

    def x_peer(d):
        return at(z, y, lax.rem(x + d, N))

    def y_peer(d):
        return at(z, lax.rem(y + d, N), x)

    z_peer = at(1 - z, y, x)
    beside = (
        {"tm": lax.rem(tm + 1, times)},
        {"tm": lax.rem(tm + times - 1, times)},
        {"sub": lax.rem(sub + 1, parts)},
        {"sub": lax.rem(sub + parts - 1, parts)},
    )
    sent = []

    def start(src, dst, peer):
        n = len(sent)
        copy = pltpu.make_async_remote_copy(
            src_ref=src,
            dst_ref=dst,
            send_sem=send_sem.at[n],
            recv_sem=recv_sem.at[n],
            device_id=peer,
            device_id_type=MESH,
        )
        sent.append(copy)
        copy.start()
        return copy

    loads = [pltpu.make_async_copy(fields.at[0, k], raw.at[k], load_sem.at[k]) for k in range(3)]
    for load in loads:
        load.start()

    barrier = pltpu.get_barrier_semaphore()
    peers = [x_peer(d) for d in FAR_FIRST] + [y_peer(d) for d in FAR_FIRST]
    peers += [z_peer] + list(beside)
    for peer in peers:
        pl.semaphore_signal(barrier, inc=1, device_id=peer, device_id_type=MESH)

    for n in range(2 * N):
        columns = slice(n * LANES, (n + 1) * LANES)
        e = weight[0, :, columns] * weight[0, :, columns]
        other = z if n < N else 1 - z
        data[n % N, other] = e
        data[n % N, 2 + other] = e * observed[0, :, columns]
    pl.semaphore_wait(barrier, len(peers))

    def begin_y(box, box_y):
        copies = [
            start(box.at[lax.rem(y + d, N)], box_y.at[y], y_peer(d)) for d in FAR_FIRST
        ]
        box_y[y] = box[y]
        return copies

    def begin_x(copies, box_y, box_t, box_x):
        for copy in copies:
            copy.wait_recv()
        for q in range(box_y.shape[1]):
            square = jnp.concatenate([box_y[n, q] for n in range(N)], axis=0)
            turned = square.T
            for n in range(N):
                box_t[n, q] = turned[n * own : (n + 1) * own]
        copies = [
            start(box_t.at[lax.rem(x + d, N)], box_x.at[x], x_peer(d)) for d in FAR_FIRST
        ]
        box_x[x] = box_t[x]
        return copies

    lane_block = lax.broadcasted_iota(jnp.int32, (own, LANES), 1) // own

    def mirrored(box_x, q, t):
        result = None
        for n in range(N):
            moved = box_x[n, q]
            if n != t:
                moved = pltpu.roll(moved, ((n - t) % N) * own, 1)
            result = moved if result is None else jnp.where(lane_block == n, moved, result)
        return result

    data_copies = begin_y(data, data_y)
    face_copies = [start(model.at[0], faces.at[n], peer) for n, peer in enumerate(beside)]

    cell_row = jnp.concatenate([model[0, j : j + 1, :] for j in range(model.shape[1])], axis=1)

    def lay_out(k):
        loads[k].wait()
        columns = slice(k * cells, (k + 1) * cells)
        for n in range(4):
            rows = slice(n * 256, (n + 1) * 256)
            flat = raw[k, rows].reshape(256, cells)
            grads[rows, columns] = flat
            weighted[rows, columns] = (flat.astype(F32) * cell_row).astype(BF16)

    def product(rows, columns):
        return lax.dot_general(
            weighted[rows, :], grads[columns, :], (((1,), (1,)), ((), ())), preferred_element_type=F32
        )

    lay_out(0)
    data_copies = begin_x(data_copies, data_y, data_t, data_x)
    lay_out(1)
    lay_out(2)

    for b in range(2):
        block = product(slice(b * 256, (b + 1) * 256), slice(half, electrodes))
        for n in range(2):
            for xx in range(N):
                piece = block[n * tile + xx * own : n * tile + (xx + 1) * own]
                pairs_a[xx, 2 * b + n] = piece
                send_a[xx, 2 * b + n] = piece.astype(BF16)
    first_a = [start(send_a.at[lax.rem(x + d, N)], recv_a.at[d - 1], x_peer(d)) for d in FAR_FIRST]

    def keep(block, block_row, block_column, row, column, place):
        r = (row - block_row) * LANES
        c = (column - block_column) * LANES
        piece = block[r : r + LANES, c : c + LANES]
        columns = slice(place * LANES, (place + 1) * LANES)
        pairs_b[row, :, columns] = piece
        send_b[row, :, columns] = piece.astype(BF16)

    for b in range(2):
        upper = product(slice(b * 256, (b + 1) * 256), slice(b * 256, half))
        lower = product(
            slice(half + b * 256, half + (b + 1) * 256), slice(half, half + (b + 1) * 256)
        )
        for row in (2 * b, 2 * b + 1):
            for column in range(N):
                if column >= row:
                    keep(upper, 2 * b, 2 * b, row, column, column)
                else:
                    keep(lower, 2 * b, 0, row, column, column)
            keep(lower, 2 * b, 0, row, row, N)
    first_b = [start(send_b.at[lax.rem(y + d, N)], recv_b.at[d - 1], y_peer(d)) for d in FAR_FIRST]

    for copy in data_copies:
        copy.wait_recv()
    low = z == 0
    nil = jnp.zeros((own, LANES), F32)
    for v in range(2):
        for t in range(N):
            data_u[v, t] = jnp.where(low, data[t, 2 * v + 1], mirrored(data_x, 2 * v + 1, t))
            direct = data[t, 2 * v]
            both = direct + mirrored(data_x, 2 * v, t)
            inside = jnp.where(low, t > y, t < y)
            corner = jnp.logical_and(low, y == t)
            data_u[v, N + t] = jnp.where(inside, both, jnp.where(corner, direct, nil))
        data_u[v, 2 * N] = jnp.where(low, nil, data[y, 2 * v])
    data_copy = start(data_u, data_z, z_peer)

    def arrived(copies, box):
        for copy in copies:
            copy.wait_recv()
        return box[0].astype(F32) + box[1].astype(F32) + box[2].astype(F32)

    acc_a[...] = pairs_a[x] + arrived(first_a, recv_a)
    second_a = [start(acc_a.at[lax.rem(y + d, N)], recv_a2.at[d - 1], y_peer(d)) for d in FAR_FIRST]
    acc_b[...] = (pairs_b[y] + arrived(first_b, recv_b)).reshape(acc_b.shape)
    second_b = [start(acc_b.at[lax.rem(x + d, N)], recv_b2.at[d - 1], x_peer(d)) for d in FAR_FIRST]

    sums = []
    third = []
    for v, (acc, mine, copies, box) in enumerate(
        ((acc_a, y, second_a, recv_a2), (acc_b, x, second_b, recv_b2))
    ):
        summed = acc[mine] + arrived(copies, box)
        potential[:, v * half : v * half + summed.shape[1]] = summed
        z_send[v, :, : summed.shape[1]] = summed.astype(BF16)
        third.append(start(z_send.at[v], z_recv.at[v], z_peer))

    scale = 1.0 / jnp.sqrt(F32(cells * 3 * parts))
    data_copy.wait_recv()

    def finish(v, tiles):
        third[v].wait_recv()
        for t in tiles:
            columns = slice(t * LANES, (t + 1) * LANES)
            inner = slice((t - v * N) * LANES, (t - v * N + 1) * LANES)
            value = (potential[:, columns] + z_recv[v, :, inner].astype(F32)) * scale
            potential[:, columns] = value
            residual = (data_u[0, t] + data_z[0, t]) * value - (data_u[1, t] + data_z[1, t])
            if v == 0:
                gather_a[x, y, :, inner] = residual.astype(BF16)
                post[t, 1] = value
            else:
                gather_b[y, x, :, inner] = residual.astype(BF16)
                if t < 2 * N:
                    post[t - N, 0] = value

    finish(0, range(N))
    level_a = [start(gather_a.at[x, y], gather_a.at[x, y], y_peer(d)) for d in FAR_FIRST]
    finish(1, range(N, 2 * N + 1))
    level_b = [start(gather_b.at[y, x], gather_b.at[y, x], x_peer(d)) for d in FAR_FIRST]
    post_copies = begin_y(post, post_y)
    for copy in level_a:
        copy.wait_recv()
    last_a = {d: start(gather_a.at[x], gather_a.at[x], x_peer(d)) for d in FAR_FIRST}
    for copy in level_b:
        copy.wait_recv()
    last_b = {d: start(gather_b.at[y], gather_b.at[y], y_peer(d)) for d in FAR_FIRST}
    post_copies = begin_x(post_copies, post_y, post_t, post_x)

    total[...] = jnp.zeros_like(total)

    def collect(matrix, columns, rows):
        made = jnp.dot(matrix, grads[columns, :], preferred_element_type=F32)
        made = made * rows.astype(F32)
        total[...] += jnp.sum(made.reshape(tile // 8, 8, terms), axis=0)

    def at_rows(first, count):
        return pl.ds(pl.multiple_of(first, count), count)

    def add_a(xx):
        rows = jnp.concatenate([grads[at_rows(yy * tile + xx * own, own), :] for yy in range(N)], axis=0)
        collect(gather_a[xx].reshape(tile, half), slice(half, electrodes), rows)

    def add_b(yy):
        matrix = gather_b[yy].reshape(tile, half + LANES)
        tiles = [matrix[:, t * LANES : (t + 1) * LANES] for t in range(N + 1)]
        none = jnp.zeros_like(tiles[0])
        upper = [jnp.where(yy <= t, tiles[t], none) for t in range(N)]
        lower = [
            jnp.where(yy > t, tiles[t], jnp.where(yy == t, tiles[N], none)) for t in range(N)
        ]
        collect(jnp.concatenate(upper, axis=1), slice(0, half), grads[at_rows(yy * tile, tile), :])
        collect(
            jnp.concatenate(lower, axis=1),
            slice(half, electrodes),
            grads[at_rows(half + yy * tile, tile), :],
        )

    add_a(x)
    add_b(y)

    for copy in post_copies:
        copy.wait_recv()
    for n in range(2 * N):
        columns = slice(n * LANES, (n + 1) * LANES)
        t = n % N
        between = potential[:, t * LANES : (t + 1) * LANES]
        within = potential[:, half + t * LANES : half + (t + 1) * LANES]
        corner = potential[:, 2 * half : 2 * half + LANES]
        turned = mirrored(post_x, 0, t)
        upper = jnp.where(y <= t, within, turned)
        lower = jnp.where(y > t, within, jnp.where(y == t, corner, turned))
        mine = jnp.where(low, upper, lower)
        others = jnp.where(low, between, mirrored(post_x, 1, t))
        here = low if n < N else z == 1
        value = jnp.where(here, mine, others)
        misfit_out[0, :, columns] = weight[0, :, columns] * (value - observed[0, :, columns])

    for d in NEAR_FIRST:
        last_a[d].wait_recv()
        add_a(lax.rem(x + N - d, N))
        last_b[d].wait_recv()
        add_b(lax.rem(y + N - d, N))

    for copy in face_copies:
        copy.wait_recv()
    centre = model[0]
    height, width = centre.shape
    lane = lax.broadcasted_iota(jnp.int32, centre.shape, 1)
    zero = jnp.zeros_like(centre)
    before_t = jnp.where(tm > 0, faces[0], zero)
    after_t = jnp.where(tm < times - 1, faces[1], zero)
    before_s = jnp.where(sub > 0, faces[2], zero)
    after_s = jnp.where(sub < parts - 1, faces[3], zero)
    near = after_t + before_t
    near = near + jnp.concatenate([centre[1:], after_s[:1]], axis=0)
    near = near + jnp.concatenate([before_s[height - 1 :], centre[: height - 1]], axis=0)
    near = near + jnp.where(lane == width - 1, 0.0, pltpu.roll(centre, width - 1, 1))
    near = near + jnp.where(lane == 0, 0.0, pltpu.roll(centre, 1, 1))
    smooth = 6.0 * centre - near
    flat = jnp.sum(total[...], axis=0, keepdims=True)
    flat = (flat[:, :cells] + flat[:, cells : 2 * cells] + flat[:, 2 * cells :]) * scale
    for j in range(height):
        gradient_out[0, j : j + 1, :] = flat[:, j * width : (j + 1) * width] + smooth[j : j + 1]

    for copy in sent:
        copy.wait_send()


def body(field_grads, model, observed, data_weight):
    electrodes = field_grads.shape[2]
    columns = field_grads.shape[3]
    width = field_grads.shape[4]
    terms = 3 * columns * width
    own = observed.shape[1]
    half = electrodes // 2
    tile = N * own
    wide = half + LANES
    dma = pltpu.SemaphoreType.DMA
    vmem = pl.BlockSpec(memory_space=pltpu.VMEM)
    return pl.pallas_call(
        kernel,
        out_shape=(
            jax.ShapeDtypeStruct(observed.shape, F32),
            jax.ShapeDtypeStruct(model.shape, F32),
        ),
        in_specs=[pl.BlockSpec(memory_space=pl.ANY)] + [vmem] * 3,
        out_specs=(vmem, vmem),
        scratch_shapes=[
            pltpu.VMEM((3, electrodes, columns, width), BF16),
            pltpu.VMEM((electrodes, terms), BF16),
            pltpu.VMEM((electrodes, terms), BF16),
            pltpu.VMEM((N, N, own, half), F32),
            pltpu.VMEM((N, tile, wide), F32),
            pltpu.VMEM((N, N, own, half), BF16),
            pltpu.VMEM((N, tile, wide), BF16),
            pltpu.VMEM((3, N, own, half), BF16),
            pltpu.VMEM((3, tile, wide), BF16),
            pltpu.VMEM((N, own, half), F32),
            pltpu.VMEM((N, own, wide), F32),
            pltpu.VMEM((3, own, half), F32),
            pltpu.VMEM((3, own, wide), F32),
            pltpu.VMEM((2, own, wide), BF16),
            pltpu.VMEM((2, own, wide), BF16),
            pltpu.VMEM((N, N, own, half), BF16),
            pltpu.VMEM((N, N, own, wide), BF16),
            pltpu.VMEM((N, 4, own, LANES), F32),
            pltpu.VMEM((N, 4, own, LANES), F32),
            pltpu.VMEM((N, 4, own, LANES), F32),
            pltpu.VMEM((N, 4, own, LANES), F32),
            pltpu.VMEM((2, 2 * N + 1, own, LANES), F32),
            pltpu.VMEM((2, 2 * N + 1, own, LANES), F32),
            pltpu.VMEM((N, 2, own, LANES), F32),
            pltpu.VMEM((N, 2, own, LANES), F32),
            pltpu.VMEM((N, 2, own, LANES), F32),
            pltpu.VMEM((N, 2, own, LANES), F32),
            pltpu.VMEM((own, 2 * half + LANES), F32),
            pltpu.VMEM((8, terms), F32),
            pltpu.VMEM((4, columns, width), F32),
            dma((3,)),
            dma((48,)),
            dma((48,)),
        ],
        compiler_params=pltpu.CompilerParams(
            collective_id=0, has_side_effects=True, vmem_limit_bytes=48 * 1024 * 1024
        ),
    )(field_grads, model, observed, data_weight)


def solution(mesh):
    return jax.shard_map(
        body,
        mesh=mesh,
        in_specs=(
            P("tm", None, None, "sub", None),
            P("tm", "sub", None),
            P("tm", "sub", None),
            P("tm", "sub", None),
        ),
        out_specs=(P("tm", "sub", None), P("tm", "sub", None)),
        check_vma=False,
    )
```

time: 586 us -> 61.5 us (0.10)
  waiting for transfers between devices: 537 us -> 0 us
  Pallas kernels: 0 us -> 54.9 us
  between operations: 14.2 us -> 0.65 us
  matrix products: 11.5 us -> 0 us
  starting transfers between devices: 8.49 us -> 0 us
  other arithmetic: 6 us -> 0 us
    psum x1 -> x0, waiting for transfers between devices: 453 us -> none  [body(): whole = lax.psum(total, 'sub')]
    all_gather x1 -> x0, waiting for transfers between devices: 81.8 us -> none  [body(): piece = lax.all_gather(back, 'sub', axis=0, tiled=True)]
    pallas_call x0 -> x1, Pallas kernels: none -> 54.9 us  [body(): pl.pallas_call(kernel, out_shape=(jax.ShapeDtypeStruct(observed.shape, F3...]
    dot_general x6 -> x0, matrix products: 11.5 us -> none  [the longest x3 5.94 us: body(): lax.dot_general(rows_k, grads_flat[k], (((1,), (1,)), ((), ())), preferre...]
    ppermute x4 -> x0, starting transfers between devices: 8.41 us -> none  [the longest x2 4.64 us: padded_2(): before = lax.ppermute(last, axis, up)]
  transfers between devices with their start and end apart: 6 -> 0, of which waited for: 3 -> 0; matrix products, arithmetic and copies ran while one was open for 1% -> 0% of each run, Pallas kernels for 0% -> 0%
where the time goes in v2:
time: 61.5 us; the launch traced here: 61.2 us
  Pallas kernels  54.9 us (89%)
  local copies, waits for them, and re-layouts  5.61 us (9%)
  between operations  0.65 us (1%)
    pallas_call x1, Pallas kernels, body(): pl.pallas_call(kernel, out_shape=(jax.ShapeDtypeStruct(observed.shape, F3...  54.9 us
    unnamed x10, local copies, waits for them, and re-layouts  5.61 us

profile of v2, /device:TPU:2, one launch (start us, length us, event | category | flops | bytes accessed | tf_op | source)
XLA Modules:
  0.0 61.2 jit_solution(1868468926229148847)
XLA Ops:
  0.6 0.0 copy-start
  0.6 1.9 %copy-done = bf16[1,3,1024,4,128]{4,3,2,1,0:T(4,128)(2,1)S(1)} copy-done((bf16[1,3,1024,4,128]{4,3,2,1,0:T(4,128)(2,1)S(1)}, bf16[1,3,1024,4,128]{4,3,2,1,0:T(4,128)(2,1)}, u32[]{:S(2)}) %copy-start) | copy-done | bytes 3145752
  2.5 0.0 copy-start.1
  2.5 0.9 %copy-done.1 = f32[1,32,1024]{2,1,0:T(8,128)S(1)} copy-done((f32[1,32,1024]{2,1,0:T(8,128)S(1)}, f32[1,32,1024]{2,1,0:T(8,128)}, u32[]{:S(2)}) %copy-start.1) | copy-done | bytes 131096
  3.4 0.0 copy-start.2
  3.4 0.9 %copy-done.2 = f32[1,32,1024]{2,1,0:T(8,128)S(1)} copy-done((f32[1,32,1024]{2,1,0:T(8,128)S(1)}, f32[1,32,1024]{2,1,0:T(8,128)}, u32[]{:S(2)}) %copy-start.2) | copy-done | bytes 131096
  4.3 0.0 copy-start.3
  4.3 0.7 %copy-done.3 = f32[1,4,128]{2,1,0:T(4,128)S(1)} copy-done((f32[1,4,128]{2,1,0:T(4,128)S(1)}, f32[1,4,128]{2,1,0:T(4,128)}, u32[]{:S(2)}) %copy-start.3) | copy-done | bytes 2072
  5.0 54.9 %shard_map.59 = (f32[1,32,1024]{2,1,0:T(8,128)S(1)}, f32[1,4,128]{2,1,0:T(4,128)S(1)}) custom-call(bf16[1,3,1024,4,128]{4,3,2,1,0:T(4,128)(2,1)S(1)} %copy-done, f32[1,4,128]{2,1,0:T(4,128)S(1)} %copy-done.3, f32[1,32,1024]{2,1,0:T(8,128)S(1)} %copy-done.1, f32[1,32,1024]{2,1,0:T(8,128)S(1)} %copy-done.2), custom_call_target="tpu_custom_call" | custom-call | tf_op jit(solution)/shard_map/pallas_call | solution.py:367
  60.0 0.7 %copy.8 = f32[1,32,1024]{2,1,0:T(8,128)} copy(f32[1,32,1024]{2,1,0:T(8,128)S(1)} %get-tuple-element.4) | data formatting | bytes 262144
  60.6 0.6 copy.9
Async XLA Ops:
  0.6 1.9 %copy-start = (bf16[1,3,1024,4,128]{4,3,2,1,0:T(4,128)(2,1)S(1)}, bf16[1,3,1024,4,128]{4,3,2,1,0:T(4,128)(2,1)}, u32[]{:S(2)}) copy-start(bf16[1,3,1024,4,128]{4,3,2,1,0:T(4,128)(2,1)} %fields.1) | copy-start | bytes 9437188
  2.5 0.9 %copy-start.1 = (f32[1,32,1024]{2,1,0:T(8,128)S(1)}, f32[1,32,1024]{2,1,0:T(8,128)}, u32[]{:S(2)}) copy-start(f32[1,32,1024]{2,1,0:T(8,128)} %observed.1) | copy-start | bytes 393220
  3.4 0.9 %copy-start.2 = (f32[1,32,1024]{2,1,0:T(8,128)S(1)}, f32[1,32,1024]{2,1,0:T(8,128)}, u32[]{:S(2)}) copy-start(f32[1,32,1024]{2,1,0:T(8,128)} %weight.1) | copy-start | bytes 393220
  4.3 0.7 %copy-start.3 = (f32[1,4,128]{2,1,0:T(4,128)S(1)}, f32[1,4,128]{2,1,0:T(4,128)}, u32[]{:S(2)}) copy-start(f32[1,4,128]{2,1,0:T(4,128)} %model.1) | copy-start | bytes 6148

commit v3 on v2

--- a/solution.py
+++ b/solution.py
@@ -17,11 +17,14 @@
 
 def kernel(
     fields,
+    model_in,
+    observed_in,
+    weight_in,
+    misfit_out,
+    gradient_out,
     model,
     observed,
     weight,
-    misfit_out,
-    gradient_out,
     raw,
     grads,
     weighted,
@@ -44,6 +47,7 @@
     data_t,
     data_x,
     data_u,
+    data_b,
     data_z,
     post,
     post_y,
@@ -102,7 +106,13 @@
         return copy
 
     loads = [pltpu.make_async_copy(fields.at[0, k], raw.at[k], load_sem.at[k]) for k in range(3)]
-    for load in loads:
+    inputs = [
+        pltpu.make_async_copy(src, dst, load_sem.at[3 + n])
+        for n, (src, dst) in enumerate(
+            ((weight_in, weight), (observed_in, observed), (model_in, model))
+        )
+    ]
+    for load in inputs + loads:
         load.start()
 
     barrier = pltpu.get_barrier_semaphore()
@@ -110,6 +120,9 @@
     peers += [z_peer] + list(beside)
     for peer in peers:
         pl.semaphore_signal(barrier, inc=1, device_id=peer, device_id_type=MESH)
+
+    for load in inputs:
+        load.wait()
 
     for n in range(2 * N):
         columns = slice(n * LANES, (n + 1) * LANES)
@@ -117,7 +130,6 @@
         other = z if n < N else 1 - z
         data[n % N, other] = e
         data[n % N, 2 + other] = e * observed[0, :, columns]
-    pl.semaphore_wait(barrier, len(peers))
 
     def begin_y(box, box_y):
         copies = [
@@ -151,9 +163,6 @@
             result = moved if result is None else jnp.where(lane_block == n, moved, result)
         return result
 
-    data_copies = begin_y(data, data_y)
-    face_copies = [start(model.at[0], faces.at[n], peer) for n, peer in enumerate(beside)]
-
     cell_row = jnp.concatenate([model[0, j : j + 1, :] for j in range(model.shape[1])], axis=1)
 
     def lay_out(k):
@@ -171,18 +180,11 @@
         )
 
     lay_out(0)
-    data_copies = begin_x(data_copies, data_y, data_t, data_x)
+    pl.semaphore_wait(barrier, len(peers))
+    data_copies = begin_y(data, data_y)
+    face_copies = [start(model.at[0], faces.at[n], peer) for n, peer in enumerate(beside)]
     lay_out(1)
     lay_out(2)
-
-    for b in range(2):
-        block = product(slice(b * 256, (b + 1) * 256), slice(half, electrodes))
-        for n in range(2):
-            for xx in range(N):
-                piece = block[n * tile + xx * own : n * tile + (xx + 1) * own]
-                pairs_a[xx, 2 * b + n] = piece
-                send_a[xx, 2 * b + n] = piece.astype(BF16)
-    first_a = [start(send_a.at[lax.rem(x + d, N)], recv_a.at[d - 1], x_peer(d)) for d in FAR_FIRST]
 
     def keep(block, block_row, block_column, row, column, place):
         r = (row - block_row) * LANES
@@ -206,6 +208,16 @@
             keep(lower, 2 * b, 0, row, row, N)
     first_b = [start(send_b.at[lax.rem(y + d, N)], recv_b.at[d - 1], y_peer(d)) for d in FAR_FIRST]
 
+    for b in range(2):
+        block = product(slice(b * 256, (b + 1) * 256), slice(half, electrodes))
+        for n in range(2):
+            for xx in range(N):
+                piece = block[n * tile + xx * own : n * tile + (xx + 1) * own]
+                pairs_a[xx, 2 * b + n] = piece
+                send_a[xx, 2 * b + n] = piece.astype(BF16)
+    first_a = [start(send_a.at[lax.rem(x + d, N)], recv_a.at[d - 1], x_peer(d)) for d in FAR_FIRST]
+    data_copies = begin_x(data_copies, data_y, data_t, data_x)
+
     for copy in data_copies:
         copy.wait_recv()
     low = z == 0
@@ -219,17 +231,18 @@
             corner = jnp.logical_and(low, y == t)
             data_u[v, N + t] = jnp.where(inside, both, jnp.where(corner, direct, nil))
         data_u[v, 2 * N] = jnp.where(low, nil, data[y, 2 * v])
-    data_copy = start(data_u, data_z, z_peer)
+    data_b[...] = data_u[...].astype(BF16)
+    data_copy = start(data_b, data_z, z_peer)
 
     def arrived(copies, box):
         for copy in copies:
             copy.wait_recv()
         return box[0].astype(F32) + box[1].astype(F32) + box[2].astype(F32)
 
+    acc_b[...] = (pairs_b[y] + arrived(first_b, recv_b)).reshape(acc_b.shape)
+    second_b = [start(acc_b.at[lax.rem(x + d, N)], recv_b2.at[d - 1], x_peer(d)) for d in FAR_FIRST]
     acc_a[...] = pairs_a[x] + arrived(first_a, recv_a)
     second_a = [start(acc_a.at[lax.rem(y + d, N)], recv_a2.at[d - 1], y_peer(d)) for d in FAR_FIRST]
-    acc_b[...] = (pairs_b[y] + arrived(first_b, recv_b)).reshape(acc_b.shape)
-    second_b = [start(acc_b.at[lax.rem(x + d, N)], recv_b2.at[d - 1], x_peer(d)) for d in FAR_FIRST]
 
     sums = []
     third = []
@@ -251,7 +264,8 @@
             inner = slice((t - v * N) * LANES, (t - v * N + 1) * LANES)
             value = (potential[:, columns] + z_recv[v, :, inner].astype(F32)) * scale
             potential[:, columns] = value
-            residual = (data_u[0, t] + data_z[0, t]) * value - (data_u[1, t] + data_z[1, t])
+            factor = data_u[0, t] + data_z[0, t].astype(F32)
+            residual = factor * value - (data_u[1, t] + data_z[1, t].astype(F32))
             if v == 0:
                 gather_a[x, y, :, inner] = residual.astype(BF16)
                 post[t, 1] = value
@@ -370,9 +384,12 @@
             jax.ShapeDtypeStruct(observed.shape, F32),
             jax.ShapeDtypeStruct(model.shape, F32),
         ),
-        in_specs=[pl.BlockSpec(memory_space=pl.ANY)] + [vmem] * 3,
+        in_specs=[pl.BlockSpec(memory_space=pltpu.HBM)] * 4,
         out_specs=(vmem, vmem),
         scratch_shapes=[
+            pltpu.VMEM(model.shape, F32),
+            pltpu.VMEM(observed.shape, F32),
+            pltpu.VMEM(observed.shape, F32),
             pltpu.VMEM((3, electrodes, columns, width), BF16),
             pltpu.VMEM((electrodes, terms), BF16),
             pltpu.VMEM((electrodes, terms), BF16),
@@ -395,7 +412,8 @@
             pltpu.VMEM((N, 4, own, LANES), F32),
             pltpu.VMEM((N, 4, own, LANES), F32),
             pltpu.VMEM((2, 2 * N + 1, own, LANES), F32),
-            pltpu.VMEM((2, 2 * N + 1, own, LANES), F32),
+            pltpu.VMEM((2, 2 * N + 1, own, LANES), BF16),
+            pltpu.VMEM((2, 2 * N + 1, own, LANES), BF16),
             pltpu.VMEM((N, 2, own, LANES), F32),
             pltpu.VMEM((N, 2, own, LANES), F32),
             pltpu.VMEM((N, 2, own, LANES), F32),
@@ -403,12 +421,12 @@
             pltpu.VMEM((own, 2 * half + LANES), F32),
             pltpu.VMEM((8, terms), F32),
             pltpu.VMEM((4, columns, width), F32),
-            dma((3,)),
+            dma((6,)),
             dma((48,)),
             dma((48,)),
         ],
         compiler_params=pltpu.CompilerParams(
-            collective_id=0, has_side_effects=True, vmem_limit_bytes=48 * 1024 * 1024
+            collective_id=0, has_side_effects=True, vmem_limit_bytes=64 * 1024 * 1024 - 65536
         ),
     )(field_grads, model, observed, data_weight)
 

time: 61.5 us -> 55.7 us (0.906)
  the two profiles are of different devices: /device:TPU:2 before, /device:TPU:1 now
where the time goes in v3:
time: 55.7 us; the launch traced here: 55.6 us
  Pallas kernels  52.1 us (94%)
  local copies, waits for them, and re-layouts  2.83 us (5%)
  between operations  0.64 us (1%)
    pallas_call x1, Pallas kernels, body(): pl.pallas_call(kernel, out_shape=(jax.ShapeDtypeStruct(observed.shape, F3...  52.1 us
    unnamed x2, local copies, waits for them, and re-layouts  2.83 us

profile of v3, /device:TPU:1, one launch (start us, length us, event | category | flops | bytes accessed | tf_op | source)
XLA Modules:
  0.0 55.6 jit_solution(15836929500083741913)
XLA Ops:
  0.6 52.1 %shard_map.59 = (f32[1,32,1024]{2,1,0:T(8,128)}, f32[1,4,128]{2,1,0:T(4,128)}) custom-call(bf16[1,3,1024,4,128]{4,3,2,1,0:T(4,128)(2,1)} %fields.1, f32[1,4,128]{2,1,0:T(4,128)} %model_in.1, f32[1,32,1024]{2,1,0:T(8,128)} %observed_in.1, f32[1,32,1024]{2,1,0:T(8,128)} %weight_in.1), custom_call_target="tpu_custom_call" | custom-call | tf_op jit(solution)/shard_map/pallas_call | solution.py:381
  52.7 1.6 %copy.8 = f32[1,32,1024]{2,1,0:T(8,128)} copy(f32[1,32,1024]{2,1,0:T(8,128)} %get-tuple-element.4) | data formatting | bytes 262144
  54.3 1.3 %copy.9 = f32[1,4,128]{2,1,0:T(4,128)} copy(f32[1,4,128]{2,1,0:T(4,128)} %get-tuple-element.5) | data formatting | bytes 4096

commit v4 on v3

--- a/solution.py
+++ b/solution.py
@@ -13,6 +13,8 @@
 LANES = 128
 FAR_FIRST = (2, 1, 3)
 NEAR_FIRST = (1, 3, 2)
+STREAMS = (("b", (0, 1, 2)), ("a", (0, 1)), ("b", (3, 4)), ("a", (2, 3)))
+BOXES = ("pairs", "send", "recv", "acc", "recv2", "z_send", "z_recv", "gather")
 
 
 def kernel(
@@ -28,20 +30,7 @@
     raw,
     grads,
     weighted,
-    pairs_a,
-    pairs_b,
-    send_a,
-    send_b,
-    recv_a,
-    recv_b,
-    acc_a,
-    acc_b,
-    recv_a2,
-    recv_b2,
-    z_send,
-    z_recv,
-    gather_a,
-    gather_b,
+    direct,
     data,
     data_y,
     data_t,
@@ -59,6 +48,7 @@
     load_sem,
     send_sem,
     recv_sem,
+    *boxes,
 ):
     electrodes, terms = grads.shape
     half = electrodes // 2
@@ -128,8 +118,9 @@
         columns = slice(n * LANES, (n + 1) * LANES)
         e = weight[0, :, columns] * weight[0, :, columns]
         other = z if n < N else 1 - z
-        data[n % N, other] = e
-        data[n % N, 2 + other] = e * observed[0, :, columns]
+        direct[n % N, other] = e
+        direct[n % N, 2 + other] = e * observed[0, :, columns]
+    data[...] = direct[...].astype(BF16)
 
     def begin_y(box, box_y):
         copies = [
@@ -142,10 +133,10 @@
         for copy in copies:
             copy.wait_recv()
         for q in range(box_y.shape[1]):
-            square = jnp.concatenate([box_y[n, q] for n in range(N)], axis=0)
+            square = jnp.concatenate([box_y[n, q].astype(F32) for n in range(N)], axis=0)
             turned = square.T
             for n in range(N):
-                box_t[n, q] = turned[n * own : (n + 1) * own]
+                box_t[n, q] = turned[n * own : (n + 1) * own].astype(box_t.dtype)
         copies = [
             start(box_t.at[lax.rem(x + d, N)], box_x.at[x], x_peer(d)) for d in FAR_FIRST
         ]
@@ -157,7 +148,7 @@
     def mirrored(box_x, q, t):
         result = None
         for n in range(N):
-            moved = box_x[n, q]
+            moved = box_x[n, q].astype(F32)
             if n != t:
                 moved = pltpu.roll(moved, ((n - t) % N) * own, 1)
             result = moved if result is None else jnp.where(lane_block == n, moved, result)
@@ -179,6 +170,16 @@
             weighted[rows, :], grads[columns, :], (((1,), (1,)), ((), ())), preferred_element_type=F32
         )
 
+    streams = []
+    for n, (kind, tiles) in enumerate(STREAMS):
+        box = dict(zip(BOXES, boxes[len(BOXES) * n : len(BOXES) * (n + 1)]))
+        if kind == "a":
+            box.update(outer=x, inner=y, outer_peer=x_peer, inner_peer=y_peer)
+        else:
+            box.update(outer=y, inner=x, outer_peer=y_peer, inner_peer=x_peer)
+        box.update(tiles=tiles, first=N * (kind == "b") + tiles[0], width=len(tiles) * LANES)
+        streams.append(box)
+
     lay_out(0)
     pl.semaphore_wait(barrier, len(peers))
     data_copies = begin_y(data, data_y)
@@ -186,13 +187,27 @@
     lay_out(1)
     lay_out(2)
 
+    def send_out(kind):
+        for (which, _), box in zip(STREAMS, streams):
+            if which == kind:
+                box["one"] = [
+                    start(box["send"].at[lax.rem(box["outer"] + d, N)], box["recv"].at[d - 1], box["outer_peer"](d))
+                    for d in FAR_FIRST
+                ]
+
+    def keep_at(kind, outer, inner, place, piece):
+        for (which, tiles), box in zip(STREAMS, streams):
+            if which == kind and place in tiles:
+                columns = slice((place - tiles[0]) * LANES, (place - tiles[0] + 1) * LANES)
+                box["pairs"][outer, inner, :, columns] = piece
+                box["send"][outer, inner, :, columns] = piece.astype(BF16)
+
     def keep(block, block_row, block_column, row, column, place):
         r = (row - block_row) * LANES
         c = (column - block_column) * LANES
         piece = block[r : r + LANES, c : c + LANES]
-        columns = slice(place * LANES, (place + 1) * LANES)
-        pairs_b[row, :, columns] = piece
-        send_b[row, :, columns] = piece.astype(BF16)
+        for xx in range(N):
+            keep_at("b", row, xx, place, piece[xx * own : (xx + 1) * own])
 
     for b in range(2):
         upper = product(slice(b * 256, (b + 1) * 256), slice(b * 256, half))
@@ -206,17 +221,17 @@
                 else:
                     keep(lower, 2 * b, 0, row, column, column)
             keep(lower, 2 * b, 0, row, row, N)
-    first_b = [start(send_b.at[lax.rem(y + d, N)], recv_b.at[d - 1], y_peer(d)) for d in FAR_FIRST]
+    send_out("b")
+    data_copies = begin_x(data_copies, data_y, data_t, data_x)
 
     for b in range(2):
         block = product(slice(b * 256, (b + 1) * 256), slice(half, electrodes))
         for n in range(2):
             for xx in range(N):
                 piece = block[n * tile + xx * own : n * tile + (xx + 1) * own]
-                pairs_a[xx, 2 * b + n] = piece
-                send_a[xx, 2 * b + n] = piece.astype(BF16)
-    first_a = [start(send_a.at[lax.rem(x + d, N)], recv_a.at[d - 1], x_peer(d)) for d in FAR_FIRST]
-    data_copies = begin_x(data_copies, data_y, data_t, data_x)
+                for t in range(N):
+                    keep_at("a", xx, 2 * b + n, t, piece[:, t * LANES : (t + 1) * LANES])
+    send_out("a")
 
     for copy in data_copies:
         copy.wait_recv()
@@ -224,13 +239,13 @@
     nil = jnp.zeros((own, LANES), F32)
     for v in range(2):
         for t in range(N):
-            data_u[v, t] = jnp.where(low, data[t, 2 * v + 1], mirrored(data_x, 2 * v + 1, t))
-            direct = data[t, 2 * v]
-            both = direct + mirrored(data_x, 2 * v, t)
+            data_u[v, t] = jnp.where(low, direct[t, 2 * v + 1], mirrored(data_x, 2 * v + 1, t))
+            plain = direct[t, 2 * v]
+            both = plain + mirrored(data_x, 2 * v, t)
             inside = jnp.where(low, t > y, t < y)
             corner = jnp.logical_and(low, y == t)
-            data_u[v, N + t] = jnp.where(inside, both, jnp.where(corner, direct, nil))
-        data_u[v, 2 * N] = jnp.where(low, nil, data[y, 2 * v])
+            data_u[v, N + t] = jnp.where(inside, both, jnp.where(corner, plain, nil))
+        data_u[v, 2 * N] = jnp.where(low, nil, direct[y, 2 * v])
     data_b[...] = data_u[...].astype(BF16)
     data_copy = start(data_b, data_z, z_peer)
 
@@ -239,52 +254,44 @@
             copy.wait_recv()
         return box[0].astype(F32) + box[1].astype(F32) + box[2].astype(F32)
 
-    acc_b[...] = (pairs_b[y] + arrived(first_b, recv_b)).reshape(acc_b.shape)
-    second_b = [start(acc_b.at[lax.rem(x + d, N)], recv_b2.at[d - 1], x_peer(d)) for d in FAR_FIRST]
-    acc_a[...] = pairs_a[x] + arrived(first_a, recv_a)
-    second_a = [start(acc_a.at[lax.rem(y + d, N)], recv_a2.at[d - 1], y_peer(d)) for d in FAR_FIRST]
-
-    sums = []
-    third = []
-    for v, (acc, mine, copies, box) in enumerate(
-        ((acc_a, y, second_a, recv_a2), (acc_b, x, second_b, recv_b2))
-    ):
-        summed = acc[mine] + arrived(copies, box)
-        potential[:, v * half : v * half + summed.shape[1]] = summed
-        z_send[v, :, : summed.shape[1]] = summed.astype(BF16)
-        third.append(start(z_send.at[v], z_recv.at[v], z_peer))
+    for box in streams:
+        box["acc"][...] = box["pairs"][box["outer"]] + arrived(box["one"], box["recv"])
+        box["two"] = [
+            start(box["acc"].at[lax.rem(box["inner"] + d, N)], box["recv2"].at[d - 1], box["inner_peer"](d))
+            for d in FAR_FIRST
+        ]
+    for box in streams:
+        summed = box["acc"][box["inner"]] + arrived(box["two"], box["recv2"])
+        potential[:, box["first"] * LANES : box["first"] * LANES + box["width"]] = summed
+        box["z_send"][...] = summed.astype(BF16)
+        box["three"] = start(box["z_send"], box["z_recv"], z_peer)
 
     scale = 1.0 / jnp.sqrt(F32(cells * 3 * parts))
     data_copy.wait_recv()
 
-    def finish(v, tiles):
-        third[v].wait_recv()
-        for t in tiles:
+    for box in streams:
+        box["three"].wait_recv()
+        block = box["gather"].at[box["outer"], box["inner"]]
+        for n in range(len(box["tiles"])):
+            t = box["first"] + n
             columns = slice(t * LANES, (t + 1) * LANES)
-            inner = slice((t - v * N) * LANES, (t - v * N + 1) * LANES)
-            value = (potential[:, columns] + z_recv[v, :, inner].astype(F32)) * scale
+            inner = slice(n * LANES, (n + 1) * LANES)
+            value = (potential[:, columns] + box["z_recv"][:, inner].astype(F32)) * scale
             potential[:, columns] = value
             factor = data_u[0, t] + data_z[0, t].astype(F32)
             residual = factor * value - (data_u[1, t] + data_z[1, t].astype(F32))
-            if v == 0:
-                gather_a[x, y, :, inner] = residual.astype(BF16)
+            block[:, inner] = residual.astype(BF16)
+            if t < N:
                 post[t, 1] = value
-            else:
-                gather_b[y, x, :, inner] = residual.astype(BF16)
-                if t < 2 * N:
-                    post[t - N, 0] = value
-
-    finish(0, range(N))
-    level_a = [start(gather_a.at[x, y], gather_a.at[x, y], y_peer(d)) for d in FAR_FIRST]
-    finish(1, range(N, 2 * N + 1))
-    level_b = [start(gather_b.at[y, x], gather_b.at[y, x], x_peer(d)) for d in FAR_FIRST]
+            elif t < 2 * N:
+                post[t - N, 0] = value
+        box["four"] = [start(block, block, box["inner_peer"](d)) for d in FAR_FIRST]
     post_copies = begin_y(post, post_y)
-    for copy in level_a:
-        copy.wait_recv()
-    last_a = {d: start(gather_a.at[x], gather_a.at[x], x_peer(d)) for d in FAR_FIRST}
-    for copy in level_b:
-        copy.wait_recv()
-    last_b = {d: start(gather_b.at[y], gather_b.at[y], y_peer(d)) for d in FAR_FIRST}
+    for box in streams:
+        for copy in box["four"]:
+            copy.wait_recv()
+        block = box["gather"].at[box["outer"]]
+        box["five"] = {d: start(block, block, box["outer_peer"](d)) for d in FAR_FIRST}
     post_copies = begin_x(post_copies, post_y, post_t, post_x)
 
     total[...] = jnp.zeros_like(total)
@@ -297,13 +304,21 @@
     def at_rows(first, count):
         return pl.ds(pl.multiple_of(first, count), count)
 
+    def gathered(kind, outer):
+        return [
+            box["gather"][outer].reshape(tile, box["width"])[:, n * LANES : (n + 1) * LANES]
+            for (which, _), box in zip(STREAMS, streams)
+            if which == kind
+            for n in range(len(box["tiles"]))
+        ]
+
     def add_a(xx):
         rows = jnp.concatenate([grads[at_rows(yy * tile + xx * own, own), :] for yy in range(N)], axis=0)
-        collect(gather_a[xx].reshape(tile, half), slice(half, electrodes), rows)
+        matrix = jnp.concatenate(gathered("a", xx), axis=1)
+        collect(matrix, slice(half, electrodes), rows)
 
     def add_b(yy):
-        matrix = gather_b[yy].reshape(tile, half + LANES)
-        tiles = [matrix[:, t * LANES : (t + 1) * LANES] for t in range(N + 1)]
+        tiles = gathered("b", yy)
         none = jnp.zeros_like(tiles[0])
         upper = [jnp.where(yy <= t, tiles[t], none) for t in range(N)]
         lower = [
@@ -337,10 +352,11 @@
         misfit_out[0, :, columns] = weight[0, :, columns] * (value - observed[0, :, columns])
 
     for d in NEAR_FIRST:
-        last_a[d].wait_recv()
-        add_a(lax.rem(x + N - d, N))
-        last_b[d].wait_recv()
-        add_b(lax.rem(y + N - d, N))
+        for kind, add, mine in (("a", add_a, x), ("b", add_b, y)):
+            for (which, _), box in zip(STREAMS, streams):
+                if which == kind:
+                    box["five"][d].wait_recv()
+            add(lax.rem(mine + N - d, N))
 
     for copy in face_copies:
         copy.wait_recv()
@@ -374,8 +390,19 @@
     terms = 3 * columns * width
     own = observed.shape[1]
     half = electrodes // 2
-    tile = N * own
-    wide = half + LANES
+    boxes = []
+    for _, tiles in STREAMS:
+        w = len(tiles) * LANES
+        boxes += [
+            pltpu.VMEM((N, N, own, w), F32),
+            pltpu.VMEM((N, N, own, w), BF16),
+            pltpu.VMEM((3, N, own, w), BF16),
+            pltpu.VMEM((N, own, w), F32),
+            pltpu.VMEM((3, own, w), F32),
+            pltpu.VMEM((own, w), BF16),
+            pltpu.VMEM((own, w), BF16),
+            pltpu.VMEM((N, N, own, w), BF16),
+        ]
     dma = pltpu.SemaphoreType.DMA
     vmem = pl.BlockSpec(memory_space=pltpu.VMEM)
     return pl.pallas_call(
@@ -393,24 +420,11 @@
             pltpu.VMEM((3, electrodes, columns, width), BF16),
             pltpu.VMEM((electrodes, terms), BF16),
             pltpu.VMEM((electrodes, terms), BF16),
-            pltpu.VMEM((N, N, own, half), F32),
-            pltpu.VMEM((N, tile, wide), F32),
-            pltpu.VMEM((N, N, own, half), BF16),
-            pltpu.VMEM((N, tile, wide), BF16),
-            pltpu.VMEM((3, N, own, half), BF16),
-            pltpu.VMEM((3, tile, wide), BF16),
-            pltpu.VMEM((N, own, half), F32),
-            pltpu.VMEM((N, own, wide), F32),
-            pltpu.VMEM((3, own, half), F32),
-            pltpu.VMEM((3, own, wide), F32),
-            pltpu.VMEM((2, own, wide), BF16),
-            pltpu.VMEM((2, own, wide), BF16),
-            pltpu.VMEM((N, N, own, half), BF16),
-            pltpu.VMEM((N, N, own, wide), BF16),
             pltpu.VMEM((N, 4, own, LANES), F32),
-            pltpu.VMEM((N, 4, own, LANES), F32),
-            pltpu.VMEM((N, 4, own, LANES), F32),
-            pltpu.VMEM((N, 4, own, LANES), F32),
+            pltpu.VMEM((N, 4, own, LANES), BF16),
+            pltpu.VMEM((N, 4, own, LANES), BF16),
+            pltpu.VMEM((N, 4, own, LANES), BF16),
+            pltpu.VMEM((N, 4, own, LANES), BF16),
             pltpu.VMEM((2, 2 * N + 1, own, LANES), F32),
             pltpu.VMEM((2, 2 * N + 1, own, LANES), BF16),
             pltpu.VMEM((2, 2 * N + 1, own, LANES), BF16),
@@ -422,9 +436,10 @@
             pltpu.VMEM((8, terms), F32),
             pltpu.VMEM((4, columns, width), F32),
             dma((6,)),
-            dma((48,)),
-            dma((48,)),
-        ],
+            dma((72,)),
+            dma((72,)),
+        ]
+        + boxes,
         compiler_params=pltpu.CompilerParams(
             collective_id=0, has_side_effects=True, vmem_limit_bytes=64 * 1024 * 1024 - 65536
         ),

time: 55.7 us -> 49.8 us (0.89)
  the two profiles are of different devices: /device:TPU:1 before, /device:TPU:2 now
where the time goes in v4:
time: 49.8 us; the launch traced here: 49.6 us
  Pallas kernels  46.2 us (93%)
  local copies, waits for them, and re-layouts  2.83 us (6%)
  between operations  0.64 us (1%)
    pallas_call x1, Pallas kernels, body(): pl.pallas_call(kernel, out_shape=(jax.ShapeDtypeStruct(observed.shape, F3...  46.2 us
    unnamed x2, local copies, waits for them, and re-layouts  2.83 us

profile of v4, /device:TPU:2, one launch (start us, length us, event | category | flops | bytes accessed | tf_op | source)
XLA Modules:
  0.0 49.6 jit_solution(7870144783394695433)
XLA Ops:
  0.6 46.2 %shard_map.59 = (f32[1,32,1024]{2,1,0:T(8,128)}, f32[1,4,128]{2,1,0:T(4,128)}) custom-call(bf16[1,3,1024,4,128]{4,3,2,1,0:T(4,128)(2,1)} %fields.1, f32[1,4,128]{2,1,0:T(4,128)} %model_in.1, f32[1,32,1024]{2,1,0:T(8,128)} %observed_in.1, f32[1,32,1024]{2,1,0:T(8,128)} %weight_in.1), custom_call_target="tpu_custom_call" | custom-call | tf_op jit(solution)/shard_map/pallas_call | solution.py:408
  46.8 1.6 %copy.8 = f32[1,32,1024]{2,1,0:T(8,128)} copy(f32[1,32,1024]{2,1,0:T(8,128)} %get-tuple-element.4) | data formatting | bytes 262144
  48.4 1.3 %copy.9 = f32[1,4,128]{2,1,0:T(4,128)} copy(f32[1,4,128]{2,1,0:T(4,128)} %get-tuple-element.5) | data formatting | bytes 4096

commit v5 on v4

--- a/solution.py
+++ b/solution.py
@@ -12,9 +12,34 @@
 NZ = 2
 LANES = 128
 FAR_FIRST = (2, 1, 3)
-NEAR_FIRST = (1, 3, 2)
-STREAMS = (("b", (0, 1, 2)), ("a", (0, 1)), ("b", (3, 4)), ("a", (2, 3)))
+STREAMS = (("b", (0, 1)), ("a", (0, 1)), ("b", (2, 3, 4)), ("a", (2, 3)))
 BOXES = ("pairs", "send", "recv", "acc", "recv2", "z_send", "z_recv", "gather")
+
+
+class Copy:
+    def __init__(self, copy, sends, receives):
+        self.copy = copy
+        self.sends = sends
+        self.receives = receives
+
+    def start(self):
+        when(self.sends, self.copy.start)
+
+    def wait_send(self):
+        when(self.sends, self.copy.wait_send)
+
+    def wait_recv(self):
+        when(self.receives, self.copy.wait_recv)
+
+
+def when(condition, action):
+    if condition is None:
+        action()
+    else:
+
+        @pl.when(condition)
+        def _():
+            action()
 
 
 def kernel(
@@ -48,6 +73,7 @@
     load_sem,
     send_sem,
     recv_sem,
+    plane_sem,
     *boxes,
 ):
     electrodes, terms = grads.shape
@@ -74,22 +100,26 @@
 
     z_peer = at(1 - z, y, x)
     beside = (
-        {"tm": lax.rem(tm + 1, times)},
-        {"tm": lax.rem(tm + times - 1, times)},
-        {"sub": lax.rem(sub + 1, parts)},
-        {"sub": lax.rem(sub + parts - 1, parts)},
+        ({"tm": lax.rem(tm + 1, times)}, tm < times - 1, tm > 0),
+        ({"tm": lax.rem(tm + times - 1, times)}, tm > 0, tm < times - 1),
+        ({"sub": lax.rem(sub + 1, parts)}, sub < parts - 1, sub > 0),
+        ({"sub": lax.rem(sub + parts - 1, parts)}, sub > 0, sub < parts - 1),
     )
     sent = []
 
-    def start(src, dst, peer):
+    def start(src, dst, peer, sends=None, receives=None):
         n = len(sent)
-        copy = pltpu.make_async_remote_copy(
-            src_ref=src,
-            dst_ref=dst,
-            send_sem=send_sem.at[n],
-            recv_sem=recv_sem.at[n],
-            device_id=peer,
-            device_id_type=MESH,
+        copy = Copy(
+            pltpu.make_async_remote_copy(
+                src_ref=src,
+                dst_ref=dst,
+                send_sem=send_sem.at[n],
+                recv_sem=recv_sem.at[n],
+                device_id=peer,
+                device_id_type=MESH,
+            ),
+            sends,
+            receives,
         )
         sent.append(copy)
         copy.start()
@@ -106,10 +136,20 @@
         load.start()
 
     barrier = pltpu.get_barrier_semaphore()
-    peers = [x_peer(d) for d in FAR_FIRST] + [y_peer(d) for d in FAR_FIRST]
-    peers += [z_peer] + list(beside)
-    for peer in peers:
-        pl.semaphore_signal(barrier, inc=1, device_id=peer, device_id_type=MESH)
+    plane = [x_peer(d) for d in FAR_FIRST] + [y_peer(d) for d in FAR_FIRST]
+
+    def greet(peer, condition=None):
+        when(
+            condition,
+            lambda: pl.semaphore_signal(barrier, inc=1, device_id=peer, device_id_type=MESH),
+        )
+
+    greet(z_peer, z == 0)
+    for peer in plane:
+        greet(peer)
+    for peer, condition, _ in beside[:2]:
+        greet(peer, condition)
+    greetings = len(plane) + z + jnp.where(tm > 0, 1, 0) + jnp.where(tm < times - 1, 1, 0)
 
     for load in inputs:
         load.wait()
@@ -122,14 +162,12 @@
         direct[n % N, 2 + other] = e * observed[0, :, columns]
     data[...] = direct[...].astype(BF16)
 
-    def begin_y(box, box_y):
-        copies = [
-            start(box.at[lax.rem(y + d, N)], box_y.at[y], y_peer(d)) for d in FAR_FIRST
-        ]
+    def begin_y(box, box_y, conditions):
+        copies = exchange(box, box_y, y, y_peer, conditions)
         box_y[y] = box[y]
         return copies
 
-    def begin_x(copies, box_y, box_t, box_x):
+    def begin_x(copies, box_y, box_t, box_x, conditions):
         for copy in copies:
             copy.wait_recv()
         for q in range(box_y.shape[1]):
@@ -137,11 +175,18 @@
             turned = square.T
             for n in range(N):
                 box_t[n, q] = turned[n * own : (n + 1) * own].astype(box_t.dtype)
-        copies = [
-            start(box_t.at[lax.rem(x + d, N)], box_x.at[x], x_peer(d)) for d in FAR_FIRST
-        ]
+        copies = exchange(box_t, box_x, x, x_peer, conditions)
         box_x[x] = box_t[x]
         return copies
+
+    def exchange(src, dst, mine, peer_of, conditions):
+        if conditions is None:
+            return [start(src.at[lax.rem(mine + d, N)], dst.at[mine], peer_of(d)) for d in FAR_FIRST]
+        return [
+            start(src.at[lax.rem(mine + d, N), q], dst.at[mine, q], peer_of(d), condition, condition)
+            for q, condition in enumerate(conditions)
+            for d in FAR_FIRST
+        ]
 
     lane_block = lax.broadcasted_iota(jnp.int32, (own, LANES), 1) // own
 
@@ -181,9 +226,19 @@
         streams.append(box)
 
     lay_out(0)
-    pl.semaphore_wait(barrier, len(peers))
-    data_copies = begin_y(data, data_y)
-    face_copies = [start(model.at[0], faces.at[n], peer) for n, peer in enumerate(beside)]
+    pl.semaphore_wait(barrier, greetings)
+    when(
+        z == 1,
+        lambda: pl.semaphore_signal(plane_sem, inc=1, device_id=z_peer, device_id_type=MESH),
+    )
+    data_copies = begin_y(data, data_y, None)
+
+    def send_faces(first):
+        return [
+            start(model.at[0], faces.at[first + n], *beside[first + n]) for n in range(2)
+        ]
+
+    face_copies = send_faces(0)
     lay_out(1)
     lay_out(2)
 
@@ -222,7 +277,7 @@
                     keep(lower, 2 * b, 0, row, column, column)
             keep(lower, 2 * b, 0, row, row, N)
     send_out("b")
-    data_copies = begin_x(data_copies, data_y, data_t, data_x)
+    data_copies = begin_x(data_copies, data_y, data_t, data_x, None)
 
     for b in range(2):
         block = product(slice(b * 256, (b + 1) * 256), slice(half, electrodes))
@@ -247,6 +302,7 @@
             data_u[v, N + t] = jnp.where(inside, both, jnp.where(corner, plain, nil))
         data_u[v, 2 * N] = jnp.where(low, nil, direct[y, 2 * v])
     data_b[...] = data_u[...].astype(BF16)
+    when(z == 0, lambda: pl.semaphore_wait(plane_sem, 1))
     data_copy = start(data_b, data_z, z_peer)
 
     def arrived(copies, box):
@@ -286,77 +342,103 @@
             elif t < 2 * N:
                 post[t - N, 0] = value
         box["four"] = [start(block, block, box["inner_peer"](d)) for d in FAR_FIRST]
-    post_copies = begin_y(post, post_y)
+    face_copies += send_faces(2)
+    post_copies = begin_y(post, post_y, (None, z == 1))
     for box in streams:
         for copy in box["four"]:
             copy.wait_recv()
         block = box["gather"].at[box["outer"]]
-        box["five"] = {d: start(block, block, box["outer_peer"](d)) for d in FAR_FIRST}
-    post_copies = begin_x(post_copies, post_y, post_t, post_x)
+        box["five"] = [start(block, block, box["outer_peer"](d)) for d in FAR_FIRST]
+    post_copies = begin_x(post_copies, post_y, post_t, post_x, (None, z == 1))
 
     total[...] = jnp.zeros_like(total)
 
-    def collect(matrix, columns, rows):
-        made = jnp.dot(matrix, grads[columns, :], preferred_element_type=F32)
-        made = made * rows.astype(F32)
-        total[...] += jnp.sum(made.reshape(tile // 8, 8, terms), axis=0)
-
-    def at_rows(first, count):
-        return pl.ds(pl.multiple_of(first, count), count)
-
-    def gathered(kind, outer):
-        return [
-            box["gather"][outer].reshape(tile, box["width"])[:, n * LANES : (n + 1) * LANES]
-            for (which, _), box in zip(STREAMS, streams)
-            if which == kind
-            for n in range(len(box["tiles"]))
+    def collect(matrix, columns, pieces):
+        count = matrix.shape[0]
+        for k in range(3):
+            span = slice(k * cells, (k + 1) * cells)
+            made = jnp.dot(matrix, grads[columns, span], preferred_element_type=F32)
+            rows = [grads[piece, span] for piece in pieces]
+            rows = rows[0] if len(rows) == 1 else jnp.concatenate(rows, axis=0)
+            made = made * rows.astype(F32)
+            total[:, span] += jnp.sum(made.reshape(count // 8, 8, cells), axis=0)
+
+    none = jnp.zeros((tile, LANES), BF16)
+
+    def stack(rows):
+        return jnp.concatenate([jnp.concatenate(row, axis=1) for row in rows], axis=0)
+
+    def add_a(box):
+        first = half + box["tiles"][0] * LANES
+        pieces = [
+            slice(yy * tile + xx * own, yy * tile + (xx + 1) * own)
+            for xx in range(N)
+            for yy in range(N)
         ]
-
-    def add_a(xx):
-        rows = jnp.concatenate([grads[at_rows(yy * tile + xx * own, own), :] for yy in range(N)], axis=0)
-        matrix = jnp.concatenate(gathered("a", xx), axis=1)
-        collect(matrix, slice(half, electrodes), rows)
-
-    def add_b(yy):
-        tiles = gathered("b", yy)
-        none = jnp.zeros_like(tiles[0])
-        upper = [jnp.where(yy <= t, tiles[t], none) for t in range(N)]
-        lower = [
-            jnp.where(yy > t, tiles[t], jnp.where(yy == t, tiles[N], none)) for t in range(N)
-        ]
-        collect(jnp.concatenate(upper, axis=1), slice(0, half), grads[at_rows(yy * tile, tile), :])
-        collect(
-            jnp.concatenate(lower, axis=1),
-            slice(half, electrodes),
-            grads[at_rows(half + yy * tile, tile), :],
-        )
-
-    add_a(x)
-    add_b(y)
-
-    for copy in post_copies:
-        copy.wait_recv()
-    for n in range(2 * N):
-        columns = slice(n * LANES, (n + 1) * LANES)
-        t = n % N
-        between = potential[:, t * LANES : (t + 1) * LANES]
-        within = potential[:, half + t * LANES : half + (t + 1) * LANES]
-        corner = potential[:, 2 * half : 2 * half + LANES]
-        turned = mirrored(post_x, 0, t)
-        upper = jnp.where(y <= t, within, turned)
-        lower = jnp.where(y > t, within, jnp.where(y == t, corner, turned))
-        mine = jnp.where(low, upper, lower)
-        others = jnp.where(low, between, mirrored(post_x, 1, t))
-        here = low if n < N else z == 1
-        value = jnp.where(here, mine, others)
-        misfit_out[0, :, columns] = weight[0, :, columns] * (value - observed[0, :, columns])
-
-    for d in NEAR_FIRST:
-        for kind, add, mine in (("a", add_a, x), ("b", add_b, y)):
-            for (which, _), box in zip(STREAMS, streams):
-                if which == kind:
-                    box["five"][d].wait_recv()
-            add(lax.rem(mine + N - d, N))
+        matrix = box["gather"][...].reshape(half, box["width"])
+        collect(matrix, slice(first, first + box["width"]), pieces)
+
+    def tiles_of(box):
+        found = {}
+        for yy in range(N):
+            rows = box["gather"][yy].reshape(tile, box["width"])
+            for n, t in enumerate(box["tiles"]):
+                found[yy, t] = rows[:, n * LANES : (n + 1) * LANES]
+        return found
+
+    def add_b(box):
+        f = tiles_of(box)
+        if box["tiles"][0] == 0:
+            collect(stack([[f[0, 0], f[0, 1]], [none, f[1, 1]]]), slice(0, 256), [slice(0, 256)])
+            collect(
+                stack([[f[1, 0], none], [f[2, 0], f[2, 1]], [f[3, 0], f[3, 1]]]),
+                slice(half, half + 256),
+                [slice(half + tile, electrodes)],
+            )
+        else:
+            collect(
+                stack([[f[0, 2], f[0, 3]], [f[1, 2], f[1, 3]], [f[2, 2], f[2, 3]], [none, f[3, 3]]]),
+                slice(256, half),
+                [slice(0, half)],
+            )
+            collect(
+                stack([[f[0, N], none], [none, f[1, N]]]),
+                slice(half, half + 256),
+                [slice(half, half + 256)],
+            )
+            collect(
+                stack([[f[2, N], none], [f[3, 2], f[3, N]]]),
+                slice(half + 256, electrodes),
+                [slice(half + 256, electrodes)],
+            )
+
+    def finish_misfit():
+        for copy in post_copies:
+            copy.wait_recv()
+        for n in range(2 * N):
+            columns = slice(n * LANES, (n + 1) * LANES)
+            t = n % N
+            between = potential[:, t * LANES : (t + 1) * LANES]
+            within = potential[:, half + t * LANES : half + (t + 1) * LANES]
+            corner = potential[:, 2 * half : 2 * half + LANES]
+            turned = mirrored(post_x, 0, t)
+            upper = jnp.where(y <= t, within, turned)
+            lower = jnp.where(y > t, within, jnp.where(y == t, corner, turned))
+            mine = jnp.where(low, upper, lower)
+            others = jnp.where(low, between, mirrored(post_x, 1, t))
+            here = low if n < N else z == 1
+            value = jnp.where(here, mine, others)
+            misfit_out[0, :, columns] = weight[0, :, columns] * (value - observed[0, :, columns])
+
+    for n, ((kind, _), box) in enumerate(zip(STREAMS, streams)):
+        for copy in box["five"]:
+            copy.wait_recv()
+        if kind == "a":
+            add_a(box)
+        else:
+            add_b(box)
+        if n == 1:
+            finish_misfit()
 
     for copy in face_copies:
         copy.wait_recv()
@@ -436,8 +518,9 @@
             pltpu.VMEM((8, terms), F32),
             pltpu.VMEM((4, columns, width), F32),
             dma((6,)),
-            dma((72,)),
-            dma((72,)),
+            dma((80,)),
+            dma((80,)),
+            pltpu.SemaphoreType.REGULAR,
         ]
         + boxes,
         compiler_params=pltpu.CompilerParams(

time: 49.8 us -> 47.8 us (0.960)
  Pallas kernels: 46.2 us -> 44.2 us
    pallas_call x1, Pallas kernels: 46.2 us -> 44.2 us  [body(): pl.pallas_call(kernel, out_shape=(jax.ShapeDtypeStruct(observed.shape, F3...]
where the time goes in v5:
time: 47.8 us; the launch traced here: 47.6 us
  Pallas kernels  44.2 us (92%)
  local copies, waits for them, and re-layouts  2.83 us (6%)
  between operations  0.64 us (1%)
    pallas_call x1, Pallas kernels, body(): pl.pallas_call(kernel, out_shape=(jax.ShapeDtypeStruct(observed.shape, F3...  44.2 us
    unnamed x2, local copies, waits for them, and re-layouts  2.83 us

profile of v5, /device:TPU:2, one launch (start us, length us, event | category | flops | bytes accessed | tf_op | source)
XLA Modules:
  0.0 47.6 jit_solution(16368482167809097044)
XLA Ops:
  0.6 44.2 %shard_map.59 = (f32[1,32,1024]{2,1,0:T(8,128)}, f32[1,4,128]{2,1,0:T(4,128)}) custom-call(bf16[1,3,1024,4,128]{4,3,2,1,0:T(4,128)(2,1)} %fields.1, f32[1,4,128]{2,1,0:T(4,128)} %model_in.1, f32[1,32,1024]{2,1,0:T(8,128)} %observed_in.1, f32[1,32,1024]{2,1,0:T(8,128)} %weight_in.1), custom_call_target="tpu_custom_call" | custom-call | tf_op jit(solution)/shard_map/pallas_call | solution.py:490
  44.8 1.6 %copy.8 = f32[1,32,1024]{2,1,0:T(8,128)} copy(f32[1,32,1024]{2,1,0:T(8,128)} %get-tuple-element.4) | data formatting | bytes 262144
  46.4 1.3 %copy.9 = f32[1,4,128]{2,1,0:T(4,128)} copy(f32[1,4,128]{2,1,0:T(4,128)} %get-tuple-element.5) | data formatting | bytes 4096

commit v6 on v5

--- a/solution.py
+++ b/solution.py
@@ -437,7 +437,7 @@
             add_a(box)
         else:
             add_b(box)
-        if n == 1:
+        if n == 3:
             finish_misfit()
 
     for copy in face_copies:

time: 47.8 us -> 47.2 us (0.987); the launches traced: 47.6 us -> 46.4 us
  Pallas kernels: 44.2 us -> 42.9 us
    pallas_call x1, Pallas kernels: 44.2 us -> 42.9 us  [body(): pl.pallas_call(kernel, out_shape=(jax.ShapeDtypeStruct(observed.shape, F3...]
where the time goes in v6:
time: 47.2 us; the launch traced here: 46.4 us
  Pallas kernels  42.9 us (91%)
  local copies, waits for them, and re-layouts  2.83 us (6%)
  between operations  0.64 us (1%)
    pallas_call x1, Pallas kernels, body(): pl.pallas_call(kernel, out_shape=(jax.ShapeDtypeStruct(observed.shape, F3...  42.9 us
    unnamed x2, local copies, waits for them, and re-layouts  2.83 us

profile of v6, /device:TPU:2, one launch (start us, length us, event | category | flops | bytes accessed | tf_op | source)
XLA Modules:
  0.0 46.4 jit_solution(14332132665354532140)
XLA Ops:
  0.6 42.9 %shard_map.59 = (f32[1,32,1024]{2,1,0:T(8,128)}, f32[1,4,128]{2,1,0:T(4,128)}) custom-call(bf16[1,3,1024,4,128]{4,3,2,1,0:T(4,128)(2,1)} %fields.1, f32[1,4,128]{2,1,0:T(4,128)} %model_in.1, f32[1,32,1024]{2,1,0:T(8,128)} %observed_in.1, f32[1,32,1024]{2,1,0:T(8,128)} %weight_in.1), custom_call_target="tpu_custom_call" | custom-call | tf_op jit(solution)/shard_map/pallas_call | solution.py:490
  43.6 1.6 %copy.8 = f32[1,32,1024]{2,1,0:T(8,128)} copy(f32[1,32,1024]{2,1,0:T(8,128)} %get-tuple-element.4) | data formatting | bytes 262144
  45.1 1.3 %copy.9 = f32[1,4,128]{2,1,0:T(4,128)} copy(f32[1,4,128]{2,1,0:T(4,128)} %get-tuple-element.5) | data formatting | bytes 4096

commit v7 on v6

--- a/solution.py
+++ b/solution.py
@@ -12,7 +12,7 @@
 NZ = 2
 LANES = 128
 FAR_FIRST = (2, 1, 3)
-STREAMS = (("b", (0, 1)), ("a", (0, 1)), ("b", (2, 3, 4)), ("a", (2, 3)))
+STREAMS = (("b", (0, 1)), ("a", (0, 1)), ("b", (2, 3)), ("a", (2, 3)), ("b", (4,)))
 BOXES = ("pairs", "send", "recv", "acc", "recv2", "z_send", "z_recv", "gather")
 
 
@@ -343,7 +343,20 @@
                 post[t - N, 0] = value
         box["four"] = [start(block, block, box["inner_peer"](d)) for d in FAR_FIRST]
     face_copies += send_faces(2)
-    post_copies = begin_y(post, post_y, (None, z == 1))
+    post_copies = []
+    for d in FAR_FIRST:
+        to, source = lax.rem(y + d, N), lax.rem(y + N - d, N)
+        post_copies.append(
+            start(
+                post.at[to, 0],
+                post_y.at[y, 0],
+                y_peer(d),
+                jnp.where(low, to - y, y - to) > 0,
+                jnp.where(low, y - source, source - y) > 0,
+            )
+        )
+        post_copies.append(start(post.at[to, 1], post_y.at[y, 1], y_peer(d), z == 1, z == 1))
+    post_y[y] = post[y]
     for box in streams:
         for copy in box["four"]:
             copy.wait_recv()
@@ -395,19 +408,21 @@
                 slice(half, half + 256),
                 [slice(half + tile, electrodes)],
             )
-        else:
+        elif box["tiles"][0] == 2:
             collect(
                 stack([[f[0, 2], f[0, 3]], [f[1, 2], f[1, 3]], [f[2, 2], f[2, 3]], [none, f[3, 3]]]),
                 slice(256, half),
                 [slice(0, half)],
             )
+            collect(f[3, 2], slice(half + 256, half + 384), [slice(half + 384, electrodes)])
+        else:
             collect(
                 stack([[f[0, N], none], [none, f[1, N]]]),
                 slice(half, half + 256),
                 [slice(half, half + 256)],
             )
             collect(
-                stack([[f[2, N], none], [f[3, 2], f[3, N]]]),
+                stack([[f[2, N], none], [none, f[3, N]]]),
                 slice(half + 256, electrodes),
                 [slice(half + 256, electrodes)],
             )
@@ -437,7 +452,7 @@
             add_a(box)
         else:
             add_b(box)
-        if n == 3:
+        if n == 4:
             finish_misfit()
 
     for copy in face_copies:
@@ -518,8 +533,8 @@
             pltpu.VMEM((8, terms), F32),
             pltpu.VMEM((4, columns, width), F32),
             dma((6,)),
-            dma((80,)),
-            dma((80,)),
+            dma((96,)),
+            dma((96,)),
             pltpu.SemaphoreType.REGULAR,
         ]
         + boxes,

time: 47.2 us -> 46.8 us (level); the launches traced: 46.4 us -> 46.6 us
  no operation moved by 1% of the time
where the time goes in v7:
time: 46.8 us; the launch traced here: 46.6 us
  Pallas kernels  43.2 us (92%)
  local copies, waits for them, and re-layouts  2.83 us (6%)
  between operations  0.64 us (1%)
    pallas_call x1, Pallas kernels, body(): pl.pallas_call(kernel, out_shape=(jax.ShapeDtypeStruct(observed.shape, F3...  43.2 us
    unnamed x2, local copies, waits for them, and re-layouts  2.83 us

profile of v7, /device:TPU:2, one launch (start us, length us, event | category | flops | bytes accessed | tf_op | source)
XLA Modules:
  0.0 46.6 jit_solution(13611598432755484145)
XLA Ops:
  0.6 43.2 %shard_map.59 = (f32[1,32,1024]{2,1,0:T(8,128)}, f32[1,4,128]{2,1,0:T(4,128)}) custom-call(bf16[1,3,1024,4,128]{4,3,2,1,0:T(4,128)(2,1)} %fields.1, f32[1,4,128]{2,1,0:T(4,128)} %model_in.1, f32[1,32,1024]{2,1,0:T(8,128)} %observed_in.1, f32[1,32,1024]{2,1,0:T(8,128)} %weight_in.1), custom_call_target="tpu_custom_call" | custom-call | tf_op jit(solution)/shard_map/pallas_call | solution.py:505
  43.8 1.6 %copy.8 = f32[1,32,1024]{2,1,0:T(8,128)} copy(f32[1,32,1024]{2,1,0:T(8,128)} %get-tuple-element.4) | data formatting | bytes 262144
  45.4 1.3 %copy.9 = f32[1,4,128]{2,1,0:T(4,128)} copy(f32[1,4,128]{2,1,0:T(4,128)} %get-tuple-element.5) | data formatting | bytes 4096
